TPU v7x, 32 devices: a whole 2x2x4 slice. The times are simulated.
32 devices in a mesh: tp: 8 (over y, x, core), dp: 4 (over z).
Axes of the slice: x: 2, y: 2, z: 4, core: 2. Of those that a mesh axis runs over, the one named last changes fastest.
Arguments:
- block_input: bfloat16 [8192, 1024], P(('tp', 'dp')), may hold values from -6 to 6
- doc_starts: int32 [8192], P('tp'), may hold values from 0 to 1, as said below
- first_gain: bfloat16 [1024], replicated, may hold values from 0.099609375 to 1.8984375
- branch_weight: bfloat16 [1024, 1536], P(None, 'dp'), may hold values from -0.1875 to 0.1875
- lru_weight: bfloat16 [1024, 1536], P(None, 'dp'), may hold values from -0.1875 to 0.1875
- filter_taps: bfloat16 [4, 1536], P(None, 'dp'), may hold values from -3 to 3
- rate_gate: bfloat16 [6, 256, 256], replicated, may hold values from -0.375 to 0.375
- input_gate: bfloat16 [6, 256, 256], replicated, may hold values from -0.375 to 0.375
- rate_bias: bfloat16 [1536], replicated, may hold values from -3 to 3
- input_bias: bfloat16 [1536], replicated, may hold values from -3 to 3
- decay_logit: bfloat16 [1536], P('dp'), may hold values from 1.5 to 7.5
- out_weight: bfloat16 [1536, 1024], P('dp'), may hold values from -0.625 to 0.625
- second_gain: bfloat16 [1024], replicated, may hold values from 0.099609375 to 1.8984375
- feed_gate: bfloat16 [1024, 3072], P(None, 'dp'), may hold values from -0.1875 to 0.1875
- feed_up: bfloat16 [1024, 3072], P(None, 'dp'), may hold values from -0.1875 to 0.1875
- feed_down: bfloat16 [3072, 1024], P('dp'), may hold values from -0.21875 to 0.21875
- cotangent: bfloat16 [8192, 1024], P(('tp', 'dp')), may hold values from -12 to 12
Outputs:
- block_output: float32 [8192, 1024], P(('tp', 'dp'))
- input_grad: float32 [8192, 1024], P(('tp', 'dp'))
- first_gain_grad: float32 [1024], replicated
- branch_weight_grad: float32 [1024, 1536], P(None, 'dp')
- lru_weight_grad: float32 [1024, 1536], P(None, 'dp')
- filter_taps_grad: float32 [4, 1536], P(None, 'dp')
- rate_gate_grad: float32 [6, 256, 256], replicated
- input_gate_grad: float32 [6, 256, 256], replicated
- rate_bias_grad: float32 [1536], replicated
- input_bias_grad: float32 [1536], replicated
- decay_logit_grad: float32 [1536], P('dp')
- out_weight_grad: float32 [1536, 1024], P('dp')
- second_gain_grad: float32 [1024], replicated
- feed_gate_grad: float32 [1024, 3072], P(None, 'dp')
- feed_up_grad: float32 [1024, 3072], P(None, 'dp')
- feed_down_grad: float32 [3072, 1024], P('dp')
Inputs may be any that keep to these rules, and one draw needn't show every extreme that they name: `doc_starts`: tokens form rows of 1024; the first token of every row is 1, and elsewhere a 1 marks a document's first token.
All inputs are finite; a program needn't handle non-finite values.
Results may differ from a plain program's by a relative error of at most 0.018.
Values may be sent and summed in bfloat16 or wider, within the bound.
A program may use at most 192 MiB of HBM per device.

v0:
```python
import math

import jax
import jax.numpy as jnp
from jax import lax
from jax.sharding import PartitionSpec as P

EPS = 1e-06
DECAY_SCALE = 8.0


def gelu_fn(value):
    return jax.nn.gelu(value, approximate=True)


def rms_norm(value, gain):
    return value * lax.rsqrt(jnp.mean(value * value, axis=-1, keepdims=True) + EPS) * gain


def delayed(signal, steps):
    if steps == 0:
        return signal
    return jnp.pad(signal, ((steps, 0), (0, 0)))[: signal.shape[0]]


def combine(earlier, later):
    return (earlier[0] * later[0], later[0] * earlier[1] + later[1])


def recurrence(carry, driven):
    length, width = carry.shape
    inner = math.gcd(length, 16)
    outer = length // inner
    carry_blocks = carry.reshape(outer, inner, width)
    driven_blocks = driven.reshape(outer, inner, width)
    running = jnp.zeros((outer, width), jnp.float32)
    factor = jnp.ones((outer, width), jnp.float32)
    states = []
    factors = []
    for place in range(inner):
        step_carry = carry_blocks[:, place]
        running = step_carry * running + driven_blocks[:, place]
        factor = step_carry * factor
        states.append(running)
        factors.append(factor)
    local_state = jnp.stack(states, axis=1)
    local_factor = jnp.stack(factors, axis=1)
    block_ends = lax.associative_scan(combine, (factor, running), axis=0)[1]
    incoming = jnp.pad(block_ends, ((1, 0), (0, 0)))[:outer]
    return (local_state + local_factor * incoming[:, None, :]).reshape(length, width)


def filtered(signal, taps, valid):
    result = taps[0] * signal
    for steps in range(1, taps.shape[0]):
        result = result + taps[steps] * delayed(signal, steps) * valid[steps]
    return result


def lru_terms(rate_logit, input_logit, decay_logit, start_col):
    decay = jnp.exp(-DECAY_SCALE * jax.nn.sigmoid(rate_logit) * jax.nn.softplus(-decay_logit))
    keep = 1.0 - start_col
    scale = (start_col + keep * jnp.sqrt(1.0 - decay * decay)) * jax.nn.sigmoid(input_logit)
    return (keep * decay, scale)


def tokens_in(stacked):
    return lax.all_gather(stacked, "dp", axis=1, tiled=True)


def tokens_out(left, right, form):
    return lax.psum_scatter(
        jnp.einsum(form, left, right, preferred_element_type=jnp.float32),
        "dp",
        scatter_dimension=0,
        tiled=True,
    )


def to_heads(stacked):
    return lax.all_to_all(stacked, "dp", split_axis=1, concat_axis=2, tiled=True)


def to_channels(stacked):
    return lax.all_to_all(stacked, "dp", split_axis=2, concat_axis=1, tiled=True)


def local(
    block_input,
    doc_starts,
    first_gain,
    branch_weight,
    lru_weight,
    filter_taps,
    rate_gate,
    input_gate,
    rate_bias,
    input_bias,
    decay_logit,
    out_weight,
    second_gain,
    feed_gate,
    feed_up,
    feed_down,
    cotangent,
):
    local_rows = block_input.shape[0]
    channels = lru_weight.shape[1]
    width_all = rate_bias.shape[0]
    heads = rate_gate.shape[0]
    block_width = rate_gate.shape[1]
    start_col = doc_starts.astype(jnp.float32)[:, None]
    keep_col = 1.0 - start_col
    valid = [jnp.ones_like(keep_col)]
    for steps in range(1, filter_taps.shape[0]):
        valid.append(valid[-1] * delayed(keep_col, steps - 1))
    taps_value = filter_taps.astype(jnp.float32)
    first_gain_value = first_gain.astype(jnp.float32)
    second_gain_value = second_gain.astype(jnp.float32)
    decay_value = decay_logit.astype(jnp.float32)
    input_value = block_input.astype(jnp.float32)
    first_local = rms_norm(input_value, first_gain_value).astype(jnp.bfloat16)
    first_full = tokens_in(first_local[None])[0]
    both_weights = jnp.concatenate([branch_weight, lru_weight], axis=1)
    projected = jnp.dot(first_full, both_weights, preferred_element_type=jnp.float32)
    branch = projected[:, :channels]
    lru_in = projected[:, channels:]
    convolved = filtered(lru_in, taps_value, valid).astype(jnp.bfloat16)
    heads_in = to_heads(convolved[None])[0].reshape(local_rows, heads, block_width)
    gate_weights = jnp.stack([rate_gate, input_gate])
    logits = jnp.einsum(
        "thi,ghio->gtho", heads_in, gate_weights, preferred_element_type=jnp.float32
    )
    bias_both = (
        jnp.stack([rate_bias, input_bias]).astype(jnp.float32).reshape(2, 1, heads, block_width)
    )
    sent_logits = (logits + bias_both).astype(jnp.bfloat16).reshape(2, local_rows, width_all)
    channel_logits = to_channels(sent_logits).astype(jnp.float32)
    carry, scale = lru_terms(channel_logits[0], channel_logits[1], decay_value, start_col)
    conv_value = convolved.astype(jnp.float32)
    state = recurrence(carry, scale * conv_value)
    gelu_branch, branch_pull = jax.vjp(gelu_fn, branch)
    product = (state * gelu_branch).astype(jnp.bfloat16)
    recurrent = tokens_out(product, out_weight, "tc,cd->td")
    residual = input_value + recurrent
    second_local = rms_norm(residual, second_gain_value).astype(jnp.bfloat16)
    second_full = tokens_in(second_local[None])[0]
    feed_cols = feed_gate.shape[1]
    feed_both = jnp.concatenate([feed_gate, feed_up], axis=1)
    gate_up = jnp.dot(second_full, feed_both, preferred_element_type=jnp.float32)
    feed_logit = gate_up[:, :feed_cols]
    up_branch = gate_up[:, feed_cols:]
    activated, gelu_pull = jax.vjp(gelu_fn, feed_logit)
    hidden = (activated * up_branch).astype(jnp.bfloat16)
    block_output = residual + tokens_out(hidden, feed_down, "tc,cd->td")
    gathered = tokens_in(jnp.stack([second_local, cotangent]))
    second_full = gathered[0]
    cot_full = gathered[1]
    hidden_grad = jnp.einsum("td,fd->tf", cot_full, feed_down, preferred_element_type=jnp.float32)
    logit_grad = gelu_pull(hidden_grad * up_branch)[0].astype(jnp.bfloat16)
    up_grad = (hidden_grad * activated).astype(jnp.bfloat16)
    grad_both = jnp.concatenate([logit_grad, up_grad], axis=1)
    both_wgrad = jnp.einsum("td,tf->df", second_full, grad_both, preferred_element_type=jnp.float32)
    gate_wgrad = both_wgrad[:, :feed_cols]
    up_wgrad = both_wgrad[:, feed_cols:]
    down_wgrad = jnp.einsum("tf,td->fd", hidden, cot_full, preferred_element_type=jnp.float32)
    second_grad = tokens_out(grad_both, feed_both, "tc,dc->td")
    _, second_pull = jax.vjp(rms_norm, residual, second_gain_value)
    residual_norm_grad, second_gain_grad = second_pull(second_grad)
    residual_grad = cotangent.astype(jnp.float32) + residual_norm_grad
    recurrent_grad = residual_grad.astype(jnp.bfloat16)
    gathered_back = tokens_in(jnp.stack([recurrent_grad, first_local]))
    back_full = gathered_back[0]
    first_full = gathered_back[1]
    out_wgrad = jnp.einsum("tc,td->cd", product, back_full, preferred_element_type=jnp.float32)
    product_grad = jnp.einsum(
        "td,cd->tc", back_full, out_weight, preferred_element_type=jnp.float32
    )
    state_grad = product_grad * gelu_branch
    branch_grad = branch_pull(product_grad * state)[0].astype(jnp.bfloat16)
    later_carry = jnp.pad(carry[1:], ((0, 1), (0, 0)))
    flow = jnp.flip(recurrence(jnp.flip(later_carry, 0), jnp.flip(state_grad, 0)), 0)
    earlier_state = delayed(state, 1)

    def terms_of(rate_logit, input_logit, decay_param):
        return lru_terms(rate_logit, input_logit, decay_param, start_col)

    _, terms_pull = jax.vjp(terms_of, channel_logits[0], channel_logits[1], decay_value)
    rate_lgrad, input_lgrad, decay_grad = terms_pull((flow * earlier_state, flow * conv_value))
    logit_grads = jnp.stack([rate_lgrad, input_lgrad]).astype(jnp.bfloat16)
    heads_grad = to_heads(logit_grads).reshape(2, local_rows, heads, block_width)
    gate_wgrads = jnp.einsum(
        "thi,gtho->ghio", heads_in, heads_grad, preferred_element_type=jnp.float32
    )
    bias_grads = jnp.sum(heads_grad.astype(jnp.float32), axis=1).reshape(2, width_all)
    heads_back = jnp.einsum(
        "ghio,gtho->thi", gate_weights, heads_grad, preferred_element_type=jnp.float32
    )
    path_back = heads_back.astype(jnp.bfloat16).reshape(1, local_rows, width_all)
    convolved_grad = flow * scale + to_channels(path_back)[0].astype(jnp.float32)

    def filter_of(signal, taps):
        return filtered(signal, taps, valid)

    _, filter_pull = jax.vjp(filter_of, lru_in, taps_value)
    lru_in_grad, taps_grad = filter_pull(convolved_grad)
    proj_grad = jnp.concatenate([branch_grad, lru_in_grad.astype(jnp.bfloat16)], axis=1)
    both_proj_wgrad = jnp.einsum(
        "td,tc->dc", first_full, proj_grad, preferred_element_type=jnp.float32
    )
    first_grad = tokens_out(proj_grad, both_weights, "tc,dc->td")
    _, first_pull = jax.vjp(rms_norm, input_value, first_gain_value)
    input_norm_grad, first_gain_grad = first_pull(first_grad)
    input_grad = residual_grad + input_norm_grad
    summed = lax.psum(
        (
            both_proj_wgrad[:, :channels],
            both_proj_wgrad[:, channels:],
            taps_grad,
            decay_grad,
            out_wgrad,
            gate_wgrad,
            up_wgrad,
            down_wgrad,
        ),
        "tp",
    )
    shared = lax.psum(
        (
            gate_wgrads[0],
            gate_wgrads[1],
            bias_grads[0],
            bias_grads[1],
            first_gain_grad,
            second_gain_grad,
        ),
        ("tp", "dp"),
    )
    return (
        block_output,
        input_grad,
        shared[4],
        summed[0],
        summed[1],
        summed[2],
        shared[0],
        shared[1],
        shared[2],
        shared[3],
        summed[3],
        summed[4],
        shared[5],
        summed[5],
        summed[6],
        summed[7],
    )


def solution(mesh):
    placed = (
        P(("tp", "dp"), None),
        P("tp"),
        P(),
        P(None, "dp"),
        P(None, "dp"),
        P(None, "dp"),
        P(),
        P(),
        P(),
        P(),
        P("dp"),
        P("dp", None),
        P(),
        P(None, "dp"),
        P(None, "dp"),
        P("dp", None),
        P(("tp", "dp"), None),
    )
    return jax.shard_map(
        local,
        mesh=mesh,
        in_specs=placed,
        out_specs=(
            P(("tp", "dp"), None),
            P(("tp", "dp"), None),
            P(),
            P(None, "dp"),
            P(None, "dp"),
            P(None, "dp"),
            P(),
            P(),
            P(),
            P(),
            P("dp"),
            P("dp", None),
            P(),
            P(None, "dp"),
            P(None, "dp"),
            P("dp", None),
        ),
        check_vma=False,
    )
```

profile of v0, /device:TPU:1, one launch (start us, length us, event | category | flops | bytes accessed | tf_op | source)
XLA Modules:
  0.0 1428.9 jit_solution(8488355787877009123)
XLA Ops:
  14.3 46.6 %all-gather.11.cloned.1.call-done = bf16[1024,1024]{1,0:T(8,128)(2,1)} async-done(((bf16[256,1024]{1,0:T(8,128)(2,1)}), bf16[1024,1024]{1,0:T(8,128)(2,1)}) %all-gather.11.cloned.1.call-update) | async-done | bytes 2097168 | tf_op jit(solution)/shard_map/all_gather | solution.py:68
  60.8 3.8 fusion.166
  70.4 7.3 reduce.9
  79.6 4.4 all-to-all-start
  88.8 15.0 %all-to-all-done = bf16[4,2,49152]{2,1,0:T(2,128)(2,1)} async-done(((bf16[4,2,49152]{2,1,0:T(2,128)(2,1)}), bf16[4,2,49152]{2,1,0:T(2,128)(2,1)}, u32[]{:S(2)}, u32[]{:S(2)}) %all-to-all-start) | async-done | bytes 786464 | tf_op jit(solution)/shard_map/all_to_all | solution.py:81
  103.8 3.7 reshape.244
  114.5 10.7 copy.386
  125.2 4.5 all-to-all-start.1
  129.9 36.3 %all-to-all-done.1 = bf16[2,256,1536]{1,0,2:T(2,128)(2,1)} async-done(((bf16[2,256,1536]{1,0,2:T(2,128)(2,1)}), bf16[2,256,1536]{1,0,2:T(2,128)(2,1)}, u32[]{:S(2)}, u32[]{:S(2)}) %all-to-all-start.1) | async-done | bytes 1572896 | tf_op jit(solution)/shard_map/all_to_all | solution.py:85
  184.4 4.1 convert_multiply_fusion.5
  293.7 3.2 fusion.167
  297.6 76.1 %reduce-scatter.5.cloned.1.call-done = f32[256,1024]{1,0:T(8,128)} async-done(((f32[1024,1024]{1,0:T(8,128)}), f32[256,1024]{1,0:T(8,128)}) %reduce-scatter.5.cloned.1.call-update) | async-done | bytes 1048592 | tf_op jit(solution)/shard_map/reduce_scatter | solution.py:72
  379.9 11.9 reduce-scatter.9.cloned.1.call-start
  395.8 28.0 %all-gather.13.cloned.1.call-done = bf16[1024,1024]{1,0:T(8,128)(2,1)} async-done(((bf16[256,1024]{1,0:T(8,128)(2,1)}), bf16[1024,1024]{1,0:T(8,128)(2,1)}) %all-gather.13.cloned.1.call-update) | async-done | bytes 2097168 | tf_op jit(solution)/shard_map/all_gather | solution.py:68
  423.8 8.6 fusion.168
  432.4 73.0 %all-gather.7.cloned.1.call-done = bf16[2,1024,1024]{2,1,0:T(8,128)(2,1)} async-done(((bf16[2,256,1024]{2,1,0:T(8,128)(2,1)}), bf16[2,1024,1024]{2,1,0:T(8,128)(2,1)}) %all-gather.7.cloned.1.call-update) | async-done | bytes 4194320 | tf_op jit(solution)/shard_map/all_gather | solution.py:68
  505.4 8.1 fusion.6
  515.3 6.9 fusion.10
  524.9 72.8 %reduce-scatter.9.cloned.1.call-done = f32[256,1024]{1,0:T(8,128)} async-done(((f32[1024,1024]{1,0:T(8,128)}), f32[256,1024]{1,0:T(8,128)}) %reduce-scatter.9.cloned.1.call-update) | async-done | bytes 1048592 | tf_op jit(solution)/shard_map/reduce_scatter | solution.py:72
  605.7 12.7 rev.10
  618.5 7.8 fusion.149
  633.3 50.9 %all-gather.9.cloned.1.call-done = bf16[2,1024,1024]{2,1,0:T(8,128)(2,1)} async-done(((bf16[2,256,1024]{2,1,0:T(8,128)(2,1)}), bf16[2,1024,1024]{2,1,0:T(8,128)(2,1)}) %all-gather.9.cloned.1.call-update) | async-done | bytes 4194320 | tf_op jit(solution)/shard_map/all_gather | solution.py:68
  684.2 6.3 fusion.27
  690.5 12.8 rev.11
  703.4 7.3 fusion.150
  810.1 12.7 rev.12
  822.9 5.4 fusion.47
  830.5 38.9 %all_to_all.48 = bf16[2,1024,384]{2,0,1:T(2,128)(2,1)S(1)} all-to-all(bf16[2,1024,384]{2,0,1:T(2,128)(2,1)S(1)} %copy.462), channel_id=1, replica_groups=mesh['tp'=8,'dp'=4] {'dp'}, dimensions={1} | all-to-all | bytes 3145728 | tf_op jit(solution)/shard_map/all_to_all | solution.py:81
  876.2 9.9 copy.1045
  886.0 10.0 reduce.10
  898.0 4.2 all-to-all-start.3
  906.5 17.4 %all-to-all-done.3 = bf16[4,2,49152]{2,1,0:T(2,128)(2,1)} async-done(((bf16[4,2,49152]{2,1,0:T(2,128)(2,1)}), bf16[4,2,49152]{2,1,0:T(2,128)(2,1)}, u32[]{:S(2)}, u32[]{:S(2)}) %all-to-all-start.3) | async-done | bytes 786464 | tf_op jit(solution)/shard_map/all_to_all | solution.py:85
  923.9 3.7 reshape.246
  930.5 3.0 copy.469
  933.5 4.3 multiply_reduce_fusion.3
  940.2 3.8 fusion.59
  945.4 3.7 fusion.169
  950.6 5.6 fusion.8
  956.2 3.7 fusion.147
  961.2 3.5 fusion.11
  972.3 15.5 %all-reduce.42 = (f32[4,384]{1,0:T(4,128)}, f32[384]{0:T(512)}) all-reduce(f32[4,384]{1,0:T(4,128)S(1)} %pad_add_fusion, f32[384]{0:T(512)S(1)} %get-tuple-element.350), channel_id=1, replica_groups=mesh['tp'=8,'dp'=4] {'tp'}, use_global_device_ids=true, to_apply=%region_16.17 | all-reduce | flops 1920 | bytes 15360 | tf_op jit(solution)/shard_map/psum | solution.py:215
  987.8 60.6 %all-reduce.47.cloned.1.call-done = (f32[6,256,256]{1,2,0:T(8,128)}, f32[6,256,256]{1,2,0:T(8,128)}) async-done(((f32[6,256,256]{1,2,0:T(8,128)}, f32[6,256,256]{1,2,0:T(8,128)}), (f32[6,256,256]{1,2,0:T(8,128)}, f32[6,256,256]{1,2,0:T(8,128)})) %all-reduce.47.cloned.1.call-update) | async-done | bytes 3145744 | tf_op jit(solution)/shard_map/psum | solution.py:228
  1051.4 3.1 copy.473
  1054.6 73.5 %reduce-scatter.11.cloned.1.call-done = f32[256,1024]{1,0:T(8,128)} async-done(((f32[1024,1024]{1,0:T(8,128)}), f32[256,1024]{1,0:T(8,128)}) %reduce-scatter.11.cloned.1.call-update) | async-done | bytes 1048592 | tf_op jit(solution)/shard_map/reduce_scatter | solution.py:72
  1129.6 44.1 %all-reduce.40 = (f32[1024]{0:T(1024)}, f32[1536]{0:T(1024)}, f32[1536]{0:T(1024)}, f32[1024]{0:T(1024)}) all-reduce(f32[1024]{0:T(1024)S(1)} %get-tuple-element.102, f32[1536]{0:T(1024)S(1)} %squeeze.298, f32[1536]{0:T(1024)S(1)} %squeeze.299, f32[1024]{0:T(1024)S(1)} %copy-done.183), channel_id=1, replica_groups=mesh['tp'=8,'dp'=4] {'tp','dp'}, use_global_device_ids=true, to_apply=%region_9.10 | all-reduce | flops 5120 | bytes 40960 | tf_op jit(solution)/shard_map/psum | solution.py:228
  1173.7 35.0 %reduce-scatter.7.cloned.1.call-done = f32[256,1024]{1,0:T(8,128)} async-done(((f32[1024,1024]{1,0:T(8,128)}), f32[256,1024]{1,0:T(8,128)}) %reduce-scatter.7.cloned.1.call-update) | async-done | bytes 1048592 | tf_op jit(solution)/shard_map/reduce_scatter | solution.py:72
  1208.7 3.8 fusion.56
  1212.5 194.4 %all-reduce.49.cloned.1.call-done = (f32[1024,384]{1,0:T(8,128)}, f32[1024,384]{1,0:T(8,128)}, f32[384,1024]{1,0:T(8,128)}, f32[1024,768]{1,0:T(8,128)}, f32[1024,768]{1,0:T(8,128)}, /*index=5*/f32[768,1024]{1,0:T(8,128)}) async-done(((f32[1024,384]{1,0:T(8,128)}, f32[1024,384]{1,0:T(8,128)}, f32[384,1024]{1,0:T(8,128)}, f32[1024,768]{1,0:T(8,128)}, f32[1024,768]{1,0:T(8,128)}, ...) | async-done | bytes 14155792 | tf_op jit(solution)/shard_map/psum | solution.py:215
  (687 shorter events, 330.0 us)
Async XLA Ops:
  7.2 498.2 %copy-start = (bf16[768,1024]{1,0:T(8,128)(2,1)S(1)}, bf16[768,1024]{1,0:T(8,128)(2,1)}, u32[]{:S(2)}) copy-start(bf16[768,1024]{1,0:T(8,128)(2,1)} %param.32) | copy-start | bytes 4718596
  7.2 53.6 %all-gather.11.cloned.1.call-start = ((), (), s32[]{:S(2)}) async-start(), calls=%async_computation.14 | async-start | bytes 2621440 | tf_op jit(solution)/shard_map/all_gather | solution.py:68
  12.7 53.6 %copy-start.169 = (f32[384]{0:T(512)}, f32[384]{0:T(512)S(1)}, u32[]{:S(2)}) copy-start(f32[384]{0:T(512)S(1)} %get-tuple-element.105) | copy-start | bytes 4612
  12.7 53.6 %copy-start.171 = (f32[384]{0:T(512)}, f32[384]{0:T(512)S(1)}, u32[]{:S(2)}) copy-start(f32[384]{0:T(512)S(1)} %get-tuple-element.106) | copy-start | bytes 4612
  12.7 53.6 %copy-start.173 = (f32[384]{0:T(512)}, f32[384]{0:T(512)S(1)}, u32[]{:S(2)}) copy-start(f32[384]{0:T(512)S(1)} %get-tuple-element.107) | copy-start | bytes 4612
  12.7 53.6 %copy-start.175 = (f32[384]{0:T(512)}, f32[384]{0:T(512)S(1)}, u32[]{:S(2)}) copy-start(f32[384]{0:T(512)S(1)} %get-tuple-element.104) | copy-start | bytes 4612
  79.6 24.2 %all-to-all-start = ((bf16[4,2,49152]{2,1,0:T(2,128)(2,1)}), bf16[4,2,49152]{2,1,0:T(2,128)(2,1)}, u32[]{:S(2)}, u32[]{:S(2)}) async-start(bf16[4,2,49152]{2,1,0:T(2,128)(2,1)} %reshape.243), calls=%async_computation | async-start | bytes 1572864 | tf_op jit(solution)/shard_map/all_to_all | solution.py:81
  125.2 41.0 %all-to-all-start.1 = ((bf16[2,256,1536]{1,0,2:T(2,128)(2,1)}), bf16[2,256,1536]{1,0,2:T(2,128)(2,1)}, u32[]{:S(2)}, u32[]{:S(2)}) async-start(bf16[2,256,1536]{1,0,2:T(2,128)(2,1)} %copy.386), calls=%async_computation.1 | async-start | bytes 3145728 | tf_op jit(solution)/shard_map/all_to_all | solution.py:85
  129.7 244.0 %reduce-scatter.5.cloned.1.call-start = ((), (), s32[]{:S(2)}) async-start(), calls=%async_computation.8 | async-start | bytes 5242880 | tf_op jit(solution)/shard_map/reduce_scatter | solution.py:72
  129.8 54.6 %copy-start.167 = (f32[1024]{0:T(1024)}, f32[1024]{0:T(1024)S(1)}, u32[]{:S(2)}) copy-start(f32[1024]{0:T(1024)S(1)} %convert_element_type.120) | copy-start | bytes 12292
  129.9 43.8 %copy-start.182 = (f32[384]{0:T(512)}, f32[384]{0:T(512)S(1)}, u32[]{:S(2)}) copy-start(f32[384]{0:T(512)S(1)} %broadcast_multiply_fusion) | copy-start | bytes 4612
  192.0 80.2 %slice-start = ((f32[64,384]{1,0:T(8,128)}), f32[1,384]{1,0:T(1,128)S(1)}, s32[]{:S(2)}) async-start(f32[64,384]{1,0:T(8,128)} %fusion.61), calls=%async_computation.18 | async-start | bytes 3072 | tf_op jit(solution)/shard_map/slice | solution.py:48
  297.0 126.8 %all-gather.13.cloned.1.call-start = ((), (), s32[]{:S(2)}) async-start(), calls=%async_computation.15 | async-start | bytes 2621440 | tf_op jit(solution)/shard_map/all_gather | solution.py:68
  297.6 302.6 %copy-start.162 = (f32[1024]{0:T(1024)}, f32[1024]{0:T(1024)S(1)}, u32[]{:S(2)}) copy-start(f32[1024]{0:T(1024)S(1)} %convert_element_type.133) | copy-start | bytes 12292
  375.3 224.9 %copy-start.177 = (f32[256]{0:T(256)}, f32[256]{0:T(256)S(1)}, u32[]{:S(2)}) copy-start(f32[256]{0:T(256)S(1)} %fusion.139) | copy-start | bytes 3076
  377.3 128.2 %all-gather.7.cloned.1.call-start = ((), (), s32[]{:S(2)}) async-start(), calls=%async_computation.10 | async-start | bytes 5242880 | tf_op jit(solution)/shard_map/all_gather | solution.py:68
  379.9 217.8 %reduce-scatter.9.cloned.1.call-start = ((), (), s32[]{:S(2)}) async-start(), calls=%async_computation.11 | async-start | bytes 5242880 | tf_op jit(solution)/shard_map/reduce_scatter | solution.py:72
  522.2 162.0 %all-gather.9.cloned.1.call-start = ((), (), s32[]{:S(2)}) async-start(), calls=%async_computation.12 | async-start | bytes 5242880 | tf_op jit(solution)/shard_map/all_gather | solution.py:68
  703.3 8.5 copy-start.31
  703.3 8.5 copy-start.37
  703.3 8.5 copy-start.43
  703.3 8.5 copy-start.50
  703.3 8.5 copy-start.60
  703.3 8.5 copy-start.72
  703.3 8.5 copy-start.78
  703.4 8.5 copy-start.88
  703.4 8.5 copy-start.98
  703.4 8.5 copy-start.108
  712.7 77.7 %slice-start.1 = ((f32[64,384]{1,0:T(8,128)}), f32[1,384]{1,0:T(1,128)S(1)}, s32[]{:S(2)}) async-start(f32[64,384]{1,0:T(8,128)} %bitcast_add_fusion.2), calls=%async_computation.19 | async-start | bytes 3072 | tf_op jit(solution)/shard_map/slice | solution.py:48
  810.1 12.7 copy-start.168
  810.1 12.7 copy-start.170
  810.1 12.7 copy-start.172
  810.1 12.7 copy-start.174
  810.1 12.8 copy-start.176
  898.0 25.9 %all-to-all-start.3 = ((bf16[4,2,49152]{2,1,0:T(2,128)(2,1)}), bf16[4,2,49152]{2,1,0:T(2,128)(2,1)}, u32[]{:S(2)}, u32[]{:S(2)}) async-start(bf16[4,2,49152]{2,1,0:T(2,128)(2,1)} %reshape.245), calls=%async_computation.6 | async-start | bytes 1572864 | tf_op jit(solution)/shard_map/all_to_all | solution.py:85
  902.2 146.2 %all-reduce.47.cloned.1.call-start = ((), (), s32[]{:S(2)}) async-start(), calls=%async_computation.16 | async-start | bytes 6291456 | tf_op jit(solution)/shard_map/psum | solution.py:228
  906.5 221.5 %reduce-scatter.11.cloned.1.call-start = ((), (), s32[]{:S(2)}) async-start(), calls=%async_computation.13 | async-start | bytes 5242880 | tf_op jit(solution)/shard_map/reduce_scatter | solution.py:72
  944.0 264.6 %reduce-scatter.7.cloned.1.call-start = ((), (), s32[]{:S(2)}) async-start(), calls=%async_computation.9 | async-start | bytes 5242880 | tf_op jit(solution)/shard_map/reduce_scatter | solution.py:72
  949.2 457.7 %all-reduce.49.cloned.1.call-start = ((), (), s32[]{:S(2)}) async-start(), calls=%async_computation.17 | async-start | bytes 28311552 | tf_op jit(solution)/shard_map/psum | solution.py:215
  1051.4 76.6 %copy-start.5 = (bf16[256,1024]{1,0:T(8,128)(2,1)S(1)}, bf16[256,1024]{1,0:T(8,128)(2,1)}, u32[]{:S(2)}) copy-start(bf16[256,1024]{1,0:T(8,128)(2,1)} %param.17) | copy-start | bytes 1572868
  1051.4 76.6 %copy-start.166 = (f32[1024]{0:T(1024)S(1)}, f32[1024]{0:T(1024)}, u32[]{:S(2)}) copy-start(f32[1024]{0:T(1024)} %copy-done.164) | copy-start | bytes 12292
  1051.4 76.6 %copy-start.181 = (f32[256]{0:T(256)S(1)}, f32[256]{0:T(256)}, u32[]{:S(2)}) copy-start(f32[256]{0:T(256)} %copy-done.179) | copy-start | bytes 3076
  1054.5 75.1 %copy-start.183 = (f32[1024]{0:T(1024)S(1)}, f32[1024]{0:T(1024)}, u32[]{:S(2)}) copy-start(f32[1024]{0:T(1024)} %get-tuple-element.99) | copy-start | bytes 12292
  1054.5 119.2 %copy-start.186 = (f32[256]{0:T(256)S(1)}, f32[256]{0:T(256)}, u32[]{:S(2)}) copy-start(f32[256]{0:T(256)} %copy-done.185) | copy-start | bytes 3076
  1054.5 154.2 %copy-start.4 = (f32[256,1024]{1,0:T(8,128)S(1)}, f32[256,1024]{1,0:T(8,128)}, u32[]{:S(2)}) copy-start(f32[256,1024]{1,0:T(8,128)} %copy-done.2) | copy-start | bytes 3145732
  1054.5 154.2 %copy-start.163 = (f32[1024]{0:T(1024)S(1)}, f32[1024]{0:T(1024)}, u32[]{:S(2)}) copy-start(f32[1024]{0:T(1024)} %copy-done.162) | copy-start | bytes 12292
  1054.5 154.2 %copy-start.178 = (f32[256]{0:T(256)S(1)}, f32[256]{0:T(256)}, u32[]{:S(2)}) copy-start(f32[256]{0:T(256)} %copy-done.177) | copy-start | bytes 3076
  1054.5 154.2 %copy-start.188 = (f32[256]{0:T(256)S(1)}, f32[256]{0:T(256)}, u32[]{:S(2)}) copy-start(f32[256]{0:T(256)} %copy-done.187) | copy-start | bytes 3076
  (170 other events, 370.9 us)
Sparse Core Ops, SparseCore 0:
  12.8 48.0 all-gather.10
  297.1 76.6 reduce-scatter.4
  377.4 46.3 all-gather.12
  425.9 79.4 all-gather.6
  522.3 75.2 reduce-scatter.8
  602.9 81.2 all-gather.8
  908.7 139.6 all-reduce.46
  1050.8 77.1 reduce-scatter.10
  1130.3 78.3 reduce-scatter.6
  1215.2 191.6 all-reduce.48
where the time goes:
time: 1450 us; the launch traced here: 1430 us
  waiting for transfers between devices  780 us (54%)
  local copies, waits for them, and re-layouts  302 us (21%)
  other arithmetic  143 us (10%)
  blocking collectives  98.5 us (7%)
  matrix products  64.5 us (4%)
  starting transfers between devices  25.6 us (2%)
  between operations  16.3 us (1%)
    reduce_scatter x4, waiting for transfers between devices, tokens_out(): lax.psum_scatter(jnp.einsum(form, left, right, preferred_element_type=jnp...  257 us
    all_gather x4, waiting for transfers between devices, tokens_in(): return lax.all_gather(stacked, 'dp', axis=1, tiled=True)  198 us
    psum x1, waiting for transfers between devices, local(): lax.psum((both_proj_wgrad[:, :channels], both_proj_wgrad[:, channels:], t...  194 us
    slice x66, local copies, waits for them, and re-layouts, recurrence(): block_ends = lax.associative_scan(combine, (factor, running), axis=0)[1]  84.8 us
    unnamed x426, local copies, waits for them, and re-layouts  65.2 us
    psum x1, waiting for transfers between devices, local(): lax.psum((gate_wgrads[0], gate_wgrads[1], bias_grads[0], bias_grads[1], f...  60.6 us
    all_to_all x2, waiting for transfers between devices, to_channels(): lax.all_to_all(stacked, 'dp', split_axis=2, concat_axis=1, tiled=True)  53.7 us
    psum x1, blocking collectives, local(): lax.psum((gate_wgrads[0], gate_wgrads[1], bias_grads[0], bias_grads[1], f...  44.1 us
  transfers between devices with their start and end apart: 13, of which 13 were waited for; matrix products, arithmetic and copies ran while one was open for 8% of the time, Pallas kernels for 0%

commit v1 on v0

v1 whole, which is shorter than its diff:
```python
import functools
import math

import jax
import jax.numpy as jnp
from jax import lax
from jax.experimental import pallas as pl
from jax.experimental.pallas import tpu as pltpu
from jax.sharding import PartitionSpec as P

EPS = 1e-06
DECAY_SCALE = 8.0
F32 = jnp.float32
BF16 = jnp.bfloat16
MESH = pl.DeviceIdType.MESH
VMEM = pltpu.VMEM
DMA = pltpu.SemaphoreType.DMA
NN = (((1,), (0,)), ((), ()))
NT = (((1,), (1,)), ((), ()))
TN = (((0,), (0,)), ((), ()))
HALO = 16
LANE = 128
GELU_A = math.sqrt(2.0 / math.pi)
GELU_B = 0.044715


def dot(left, right, form):
    return lax.dot_general(left, right, form, preferred_element_type=F32)


def sigmoid(v):
    return 1.0 / (1.0 + jnp.exp(-v))


def softplus(v):
    return jnp.maximum(v, 0.0) + jnp.log1p(jnp.exp(-jnp.abs(v)))


def gelu_both(v):
    square = v * v
    tanh = jnp.tanh(GELU_A * v * (1.0 + GELU_B * square))
    half = 0.5 * (1.0 + tanh)
    slope = half + 0.5 * v * (1.0 - tanh * tanh) * (GELU_A * (1.0 + 3.0 * GELU_B * square))
    return v * half, slope


def gelu_only(v):
    return v * (0.5 * (1.0 + jnp.tanh(GELU_A * v * (1.0 + GELU_B * v * v))))


class Place:
    def __init__(self, nz):
        self.nz = nz
        self.t = lax.axis_index("tp")
        self.z = lax.axis_index("dp")
        self.b = lax.rem(self.t, 8)
        self.core = lax.rem(self.t, 2)
        self.x = lax.rem(self.t // 2, 2)
        self.y = lax.rem(self.t // 4, 2)
        self.chip = self.b // 2

    def flip(self, r):
        t = self.t
        if r & 1:
            t = t + 2 - 4 * self.x
        if r & 2:
            t = t + 4 - 8 * self.y
        return t

    def chip_of(self, r):
        c = self.chip
        if r & 1:
            c = c + 1 - 2 * self.x
        if r & 2:
            c = c + 2 - 4 * self.y
        return c

    def plane(self, r):
        return (self.flip(r), self.z)

    def sibling(self):
        return (self.t + 1 - 2 * self.core, self.z)

    def along(self, d):
        return (self.t, lax.rem(self.z + d, self.nz))

    def z_from(self, d):
        return lax.rem(self.z + self.nz - d, self.nz)


def greet(peers):
    barrier = pltpu.get_barrier_semaphore()
    for peer in peers:
        pl.semaphore_signal(barrier, inc=1, device_id=peer, device_id_type=MESH)
    pl.semaphore_wait(barrier, len(peers))


def remote(src, dst, send, recv, peer):
    return pltpu.make_async_remote_copy(
        src_ref=src, dst_ref=dst, send_sem=send, recv_sem=recv, device_id=peer, device_id_type=MESH
    )


class Sends:
    def __init__(self):
        self.started = []

    def when(self, cond, action):
        if cond is None:
            action()
        else:
            pl.when(cond)(action)

    def go(self, make, cond=None):
        self.when(cond, lambda: make().start())
        self.started.append((cond, make))

    def arrived(self, make, cond=None):
        self.when(cond, lambda: make().wait_recv())

    def sent(self, make):
        make().wait_send()
        self.started = [(cond, other) for cond, other in self.started if other is not make]

    def finish(self):
        for cond, make in self.started:
            self.when(cond, lambda: make().wait_send())


class PlaneGather:
    def __init__(self, me, out, piece, send, recv, at, cond=None, first=None, siblings=True):
        self.me, self.out, self.piece, self.cond, self.siblings = me, out, piece, cond, siblings
        self.send, self.recv, self.at, self.first = send, recv, at, first

    def copy(self, i, src, dst, peer):
        return remote(src, dst, self.send.at[self.at + (i,)], self.recv.at[self.at + (i,)], peer)

    def whole(self, i, r, peer, first=False):
        def make():
            place = self.piece(self.me.chip_of(r), self.me.core, None)
            return self.copy(i, self.first() if first and self.first else place, place, peer)
        return make

    def half(self, i, r, part, peer):
        def make():
            place = self.piece(self.me.chip_of(r), self.me.core, part)
            return self.copy(i, place, place, peer)
        return make

    def begin(self):
        for i, r in ((0, 1), (1, 2)):
            self.out.go(self.whole(i, 0, self.me.plane(r), True), self.cond)
        if self.siblings:
            self.out.go(self.whole(4, 0, self.me.sibling(), True), self.cond)

    def relay(self):
        me = self.me
        for i, r, part in ((0, 1, 0), (1, 2, 1)):
            self.out.arrived(self.whole(i, r, me.plane(r)), self.cond)
            self.out.go(self.half(2 + i, r, part, me.plane(3 - r)), self.cond)
            if self.siblings:
                self.out.go(self.whole(4 + r, r, me.sibling()), self.cond)

    def far(self):
        for part in (0, 1):
            self.out.arrived(self.half(2 + part, 3, part, self.me.plane(2 - part)), self.cond)
        if self.siblings:
            self.out.go(self.whole(7, 3, self.me.sibling()), self.cond)

    def end(self):
        if not self.siblings:
            return
        me = self.me
        for r in range(4):
            def make(r=r):
                place = self.piece(me.chip_of(r), 1 - me.core, None)
                return self.copy(4 + r, place, place, me.sibling())
            self.out.arrived(make, self.cond)


class PlaneSum:
    def __init__(self, me, out, block, recv, send_sem, recv_sem, at, source=None):
        self.me, self.out, self.block, self.got = me, out, block, recv
        self.send_sem, self.recv_sem, self.at = send_sem, recv_sem, at
        self.source = source or block

    def copy(self, i, src, peer):
        def make():
            return remote(
                src(), self.got(i), self.send_sem.at[self.at + (i,)], self.recv_sem.at[self.at + (i,)], peer
            )
        return make

    def begin(self):
        for half, r in ((0, 1), (1, 2)):
            for i, to in ((1, 3), (0, r)):
                self.out.go(self.copy(2 * half + i, lambda to=to, half=half: self.source(to, half), self.me.plane(r)))

    def wait(self, i):
        self.out.arrived(self.copy(i, lambda: self.got(i), self.me.plane(1)))

    def relay(self):
        for half, r in ((0, 2), (1, 1)):
            self.wait(2 * half + 1)
            mine = self.block(r, half)
            mine[...] = (mine[...].astype(F32) + self.got(2 * half + 1)[...].astype(F32)).astype(BF16)
            self.out.go(self.copy(4 + half, lambda r=r, half=half: self.block(r, half), self.me.plane(r)))

    def total(self, half):
        self.wait(2 * half)
        self.wait(4 + half)
        return self.got(2 * half)[...].astype(F32) + self.got(4 + half)[...].astype(F32)


def rows(i, size):
    return pl.ds(pl.multiple_of(i * size, size), size)


def rms(v, gain):
    return v * lax.rsqrt(jnp.mean(v * v, axis=-1, keepdims=True) + EPS) * gain


def head_lanes(h, width):
    return pl.ds(pl.multiple_of(h * width, width), width)


def tile_scan(a, b, row, back):
    for step in (1, 2, 4):
        if back:
            seen = row < 8 - step
            shift = 8 - step
        else:
            seen = row >= step
            shift = step
        b_before = jnp.where(seen, pltpu.roll(b, shift, 0), 0.0)
        a_before = jnp.where(seen, pltpu.roll(a, shift, 0), 1.0)
        b = b + a * b_before
        a = a * a_before
    return a, b


def forward_kernel(nz, heads, x, vecs, rg, ig, cot, lw, bw, ow, fgate, fup, fdown,
                   o_wl, o_wb, o_wo, o_fb, o_lin, o_br, o_cv, o_rl, o_il, o_st, o_pr, o_y, o_wg,
                   sin, mk, vec, base, rgrad, g2g,
                   wl, wb, wo, f, cots, win, turned, fb, lin, br, cv, rl, il, st, pr, pst, ends, ms, hx,
                   res, s, h, lg, ug, ybuf, sbuf, srecv, sown,
                   lsem, osem, zs, zr, ps, pr_sem, fcs, fcr, qs, qr, vs, vr, es, er, hs, hr, ss, sr, gs, gr):
    me = Place(nz)
    out, feeds = Sends(), Sends()
    tokens, model = x.shape
    lru = wl.shape[1]
    width = lru // heads
    own = lru // nz
    cols = f.shape[1]
    part = cols // (2 * nz)
    piece_rows = model // 8
    chunk = 256
    z = me.z

    window = pl.ds(pl.multiple_of((me.chip // 2) * (4 * part) + lax.rem(me.chip, 2) * LANE, LANE), 256)
    shift = 64 * lax.rem(me.chip, 2)
    mine = rows(z, own)
    local = [
        (fgate.at[:, window], win.at[0]),
        (fup.at[:, window], win.at[1]),
        (lw, wl.at[:, mine]),
        (bw, wb.at[:, mine]),
        (ow, wo.at[mine]),
        (fdown.at[rows(me.chip, 2 * part)], f.at[2, rows(z, 2 * part)]),
        (cot, cots.at[0]),
    ]
    local = [pltpu.make_async_copy(a, b, lsem.at[i]) for i, (a, b) in enumerate(local)]
    for copy in local:
        copy.start()
    greet([me.along(d) for d in range(1, nz)] + [me.plane(r) for r in (1, 2, 3)] + [me.sibling()])

    def vector(d, origin):
        def make():
            place = vec.at[:, rows(origin(), own)]
            return remote(vecs.at[8:16, 0:own], place, vs.at[d - 1], vr.at[d - 1], me.along(d))
        return make

    def halo():
        return remote(x.at[tokens - HALO:tokens], hx, hs.at[0], hr.at[0], me.along(1))

    out.go(halo)
    for d in range(1, nz):
        out.go(vector(d, lambda: z))

    def slot(m, zz, b):
        if m < 2:
            return (wl, wb)[m].at[rows(b, piece_rows), rows(zz, own)]
        if m == 2:
            return wo.at[rows(zz, own), rows(b, LANE)]
        at = pl.ds(pl.multiple_of(zz * (2 * part) + me.core * part, part), part)
        return f.at[0:2, at] if m == 3 else f.at[2, at]

    def source(m):
        if m < 2:
            return (lw, bw)[m].at[rows(me.b, piece_rows)]
        if m == 2:
            return ow.at[:, rows(me.b, LANE)]
        if m == 3:
            return turned.at[:, pl.ds(pl.multiple_of(shift + me.core * part, 32), part)]
        return fdown.at[pl.ds(pl.multiple_of(me.chip * (2 * part) + me.core * part, part), part)]

    def origin(hop, right):
        return z - 1 - hop if right else z + 1 + hop

    def has(hop, right):
        return z - 1 - hop >= 0 if right else z + 1 + hop < nz

    def along(m, hop, right, from_me):
        def make():
            step = 1 if right else -1
            zz = z - step * hop if from_me else origin(hop, right)
            place = slot(m, zz, me.b)
            src = source(m) if from_me and hop == 0 else place
            at = (m, hop, int(right))
            peer = (me.t, z + step if from_me else z)
            return remote(src, place, zs.at[at], zr.at[at], peer)
        return make

    def z_begin(m, hop=0):
        for right in (True, False):
            there = z + 1 < nz if right else z >= 1
            if hop:
                there = jnp.logical_and(there, has(hop - 1, right))
            (out if m < 3 else feeds).go(along(m, hop, right, True), there)

    gathers = {}
    for m in range(3):
        for hop in range(nz - 1):
            for right in (True, False):
                def place(chip, core, half, m=m, hop=hop, right=right):
                    zz, b = origin(hop, right), 2 * chip + core
                    if half is None:
                        return slot(m, zz, b)
                    if m < 2:
                        at = pl.ds(pl.multiple_of(b * piece_rows + half * (piece_rows // 2), piece_rows // 2), piece_rows // 2)
                        return (wl, wb)[m].at[at, rows(zz, own)]
                    at = pl.ds(pl.multiple_of(zz * own + half * (own // 2), own // 2), own // 2)
                    return wo.at[at, rows(b, LANE)]
                gathers[m, hop, right] = PlaneGather(
                    me, out, place, ps, pr_sem, (m, 2 * hop + int(right)), has(hop, right)
                )

    def share(m, hop, right, from_me):
        def make():
            at = (m - 3, 2 * hop + int(right))
            place = slot(m, origin(hop, right), me.b)
            if not from_me:
                other = pl.ds(pl.multiple_of(origin(hop, right) * (2 * part) + (1 - me.core) * part, part), part)
                place = f.at[0:2, other] if m == 3 else f.at[2, other]
            return remote(place, place, fcs.at[at], fcr.at[at], me.sibling())
        return make

    def z_step(m, hop):
        for right in (True, False):
            out.arrived(along(m, hop, right, False), has(hop, right))
        if hop + 1 < nz - 1:
            z_begin(m, hop + 1)
        for right in (True, False):
            if m < 3:
                gathers[m, hop, right].begin()
            else:
                feeds.go(share(m, hop, right, True), has(hop, right))

    def relay(m, hop):
        for right in (True, False):
            gathers[m, hop, right].relay()

    def far(m, hop):
        for right in (True, False):
            gathers[m, hop, right].far()

    def all_of(m):
        for hop in range(nz - 1):
            for right in (True, False):
                gathers[m, hop, right].end()

    cot_half = tokens // 2

    def cot_whole(i, r):
        return lambda: remote(cot, cots.at[r], qs.at[i], qr.at[i], me.plane(r))

    def cot_part(half, r):
        at = pl.ds(half * cot_half, cot_half)
        return lambda: remote(cots.at[r, at], cots.at[3, at], qs.at[2 + half], qr.at[2 + half], me.plane(3 - r))

    z_begin(0)
    for i, r in ((0, 1), (1, 2)):
        out.go(cot_whole(i, r))

    length = nz * tokens
    lane = lax.broadcasted_iota(jnp.int32, (1, length), 1)
    start_row = vecs[4:5, 0:length]
    keep_row = 1.0 - start_row
    valid = keep_row
    lines, later_lines = [start_row, valid], []
    for k in range(1, 4):
        if k > 1:
            valid = valid * jnp.where(lane >= k - 1, pltpu.roll(keep_row, k - 1, 1), 0.0)
            lines.append(valid)
        later_lines.append(jnp.where(lane < length - k, pltpu.roll(valid, length - k, 1), 0.0))
    ms[...] = jnp.concatenate(lines + later_lines + [jnp.zeros_like(start_row)], axis=0)
    mk[...] = jnp.concatenate([ms[:, rows(z, tokens)], jnp.zeros((LANE - 8, tokens), F32)], axis=0).T
    g1, g2 = vecs[0:1, 0:model], vecs[1:2, 0:model]
    fb[HALO:] = rms(x[...].astype(F32), g1).astype(BF16)
    for i in range(2):
        local[i].wait()
        turned[i] = win[i].T
    own_turned = pltpu.make_async_copy(
        turned.at[:, pl.ds(pl.multiple_of(shift, 32), 2 * part)], f.at[0:2, rows(z, 2 * part)], lsem.at[7]
    )
    own_turned.start()
    out.arrived(halo)
    fb[0:HALO] = rms(hx[...].astype(F32), g1).astype(BF16)

    z_step(0, 0)
    z_begin(1)
    z_step(0, 1)
    z_step(1, 0)
    z_begin(2)
    relay(0, 0)
    z_step(0, 2)
    z_step(1, 1)
    z_step(2, 0)
    z_begin(3)
    relay(0, 1)
    relay(1, 0)
    z_step(1, 2)
    z_step(2, 1)
    z_begin(4)
    for i, r in ((0, 1), (1, 2)):
        out.arrived(cot_whole(i, r))
        out.go(cot_part(i, r))
    far(0, 0)
    relay(0, 2)
    relay(1, 1)
    relay(2, 0)
    z_step(2, 2)
    far(0, 1)
    far(0, 2)
    for d in range(1, nz):
        out.arrived(vector(d, lambda: me.z_from(d)))
    vec[:, mine] = vecs[8:16, 0:own]
    for i in range(2, 7):
        local[i].wait()
    all_of(0)

    def lanes(h):
        return head_lanes(h, width)

    def project(h, _):
        lin[h] = dot(fb[...], wl[:, lanes(h)], NN)
        taps = vec[0:4, lanes(h)]
        conv = taps[0:1] * lin[h, HALO:, :]
        for k in range(1, 4):
            conv = conv + taps[k:k + 1] * lin[h, HALO - k:HALO - k + tokens, :] * mk[:, k:k + 1]
        conv = conv.astype(BF16)
        cv[h] = conv
        rl[h] = (dot(conv, rg[h], NN) + vecs[2:3, lanes(h)]).astype(BF16)
        il[h] = (dot(conv, ig[h], NN) + vecs[3:4, lanes(h)]).astype(BF16)
        return 0

    lax.fori_loop(0, heads, project, 0)
    relay(1, 2)
    relay(2, 1)
    far(1, 0)
    far(1, 1)
    relay(2, 2)
    row = lax.broadcasted_iota(jnp.int32, (8, width), 0)

    def scan_head(h, _):
        rate = softplus(-vec[4:5, lanes(h)]) * -DECAY_SCALE

        def tile(i, carried):
            state, factor = carried
            at = rows(i, 16)
            start = mk[at, 0:1]
            keep = 1.0 - start
            decay = jnp.exp(sigmoid(rl[h, at, :].astype(F32)) * rate)
            a = keep * decay
            scale = (start + keep * jnp.sqrt(1.0 - decay * decay)) * sigmoid(il[h, at, :].astype(F32))
            b = scale * cv[h, at, :].astype(F32)
            for t in range(2):
                cum, run = tile_scan(a[8 * t:8 * t + 8], b[8 * t:8 * t + 8], row, False)
                run = run + cum * state
                cum = cum * factor
                here = pl.ds(pl.multiple_of(i * 16 + 8 * t, 8), 8)
                st[h, here, :] = run
                pst[h, here, :] = cum
                state, factor = run[7:8], cum[7:8]
            return state, factor

        state, factor = lax.fori_loop(
            0, tokens // 16, tile, (jnp.zeros((1, width), F32), jnp.ones((1, width), F32))
        )
        ends[0, 0:1, lanes(h)] = state
        ends[0, 1:2, lanes(h)] = factor
        return 0

    lax.fori_loop(0, heads, scan_head, 0)

    def end_copy(d):
        return lambda: remote(ends.at[0], ends.at[d], es.at[d - 1], er.at[d - 1], me.along(d))

    for d in range(1, nz):
        out.go(end_copy(d))
    far(1, 2)
    all_of(1)

    def branch(h, _):
        br[h] = dot(fb[HALO:], wb[:, lanes(h)], NN)
        return 0

    lax.fori_loop(0, heads, branch, 0)
    z_step(3, 0)
    for hop in range(nz - 1):
        far(2, hop)
    for d in range(1, nz):
        out.arrived(end_copy(d))
    incoming = jnp.zeros((1, lru), F32)
    for d in range(nz - 1, 0, -1):
        end = ends[d, 0:1, :] + ends[d, 1:2, :] * incoming
        incoming = jnp.where(d <= z, end, incoming)
    sin[...] = incoming

    def finish(h, _):
        state = st[h] + pst[h] * sin[:, lanes(h)]
        st[h] = state
        pr[:, lanes(h)] = (state * gelu_only(br[h])).astype(BF16)
        return 0

    lax.fori_loop(0, heads, finish, 0)
    z_step(3, 1)
    all_of(2)

    def project_out(j, _):
        at = rows(j, chunk)
        res[:, at] = x[:, at].astype(F32) + dot(pr[...], wo[:, at], NN)
        return 0

    lax.fori_loop(0, model // chunk, project_out, 0)
    s[0:tokens] = rms(res[...], g2).astype(BF16)

    def second_copy(r):
        return lambda: remote(s.at[0:tokens], s.at[r * tokens:(r + 1) * tokens], ss.at[r - 1], sr.at[r - 1], me.plane(r))

    for r in (1, 2, 3):
        out.go(second_copy(r))
    saved = [
        (wl, o_wl), (wb, o_wb), (wo, o_wo), (fb, o_fb), (lin, o_lin), (br, o_br), (cv, o_cv), (rl, o_rl), (il, o_il),
        (st, o_st), (pr, o_pr),
    ]
    saved = [pltpu.make_async_copy(a, b, osem.at[i]) for i, (a, b) in enumerate(saved)]
    for copy in saved:
        copy.start()
    z_step(3, 2)
    for hop in range(nz - 1):
        z_step(4, hop)
    for m in (3, 4):
        for hop in range(nz - 1):
            for right in (True, False):
                out.arrived(share(m, hop, right, False), has(hop, right))
    own_turned.wait()
    for half, r in ((0, 2), (1, 1)):
        out.arrived(cot_part(half, r))

    def sum_copy(r):
        return lambda: remote(sbuf.at[r - 1], srecv.at[r - 1], gs.at[r - 1], gr.at[r - 1], me.plane(r))

    for r in range(4):
        if r:
            out.arrived(second_copy(r))
        at = pl.ds(r * tokens, tokens)

        def hidden_of(j, _):
            here = rows(j, chunk)
            second = s[at]
            act, slope = gelu_both(dot(second, f[0, here, :], NT))
            up = dot(second, f[1, here, :], NT)
            h[at, here] = (act * up).astype(BF16)
            hg = dot(cots[r], f[2, here, :], NT)
            lg[at, here] = (hg * up * slope).astype(BF16)
            ug[at, here] = (hg * act).astype(BF16)
            return 0

        lax.fori_loop(0, cols // chunk, hidden_of, 0)

        def back_of(j, _):
            here = rows(j, chunk)
            value = dot(lg[at], f[0, :, here], NN) + dot(ug[at], f[1, :, here], NN)
            if r:
                sbuf[r - 1, :, here] = value.astype(BF16)
            else:
                sown[:, here] = value
            return 0

        lax.fori_loop(0, model // chunk, back_of, 0)
        if r:
            out.go(sum_copy(r))

    def out_of(j, _):
        here = rows(j, chunk)
        for r in range(4):
            value = dot(h[r * tokens:(r + 1) * tokens], f[2, :, here], NN)
            if r:
                ybuf[r - 1, :, here] = value.astype(BF16)
            else:
                base[:, here] = res[:, here] + value
        return 0

    lax.fori_loop(0, model // chunk, out_of, 0)
    last = [pltpu.make_async_copy(ybuf, o_y, osem.at[11])]
    last[0].start()

    def wgrads(i, _):
        here = rows(i, chunk)
        for j in range(cols // chunk):
            at = pl.ds(j * chunk, chunk)
            f[0, at, here] = dot(lg[:, j * chunk:(j + 1) * chunk], s[:, here], TN).astype(BF16)
            f[1, at, here] = dot(ug[:, j * chunk:(j + 1) * chunk], s[:, here], TN).astype(BF16)
            other = jnp.concatenate([cots[r, :, here] for r in range(4)], axis=0)
            f[2, at, here] = dot(h[:, j * chunk:(j + 1) * chunk], other, TN).astype(BF16)
        return 0

    feeds.finish()
    lax.fori_loop(0, model // chunk, wgrads, 0)
    last.append(pltpu.make_async_copy(f, o_wg, osem.at[12]))
    last[1].start()
    for r in (1, 2, 3):
        out.arrived(sum_copy(r))
    sg = sown[...]
    for r in range(3):
        sg = sg + srecv[r].astype(F32)
    value = res[...]
    q = sg * g2
    inv = lax.rsqrt(jnp.mean(value * value, axis=-1, keepdims=True) + EPS)
    pull = jnp.mean(q * value, axis=-1, keepdims=True)
    rgrad[...] = cots[0].astype(F32) + (inv * q - value * (inv * inv * inv * pull))
    g2g[...] = jnp.sum(sg * value * inv, axis=0, keepdims=True)
    for copy in saved + last:
        copy.wait()
    out.finish()


def forward(nz, x, vecs, rg, ig, cot, lw, bw, ow, fgate, fup, fdown):
    tokens, model = x.shape
    heads, width = rg.shape[0], rg.shape[1]
    lru = heads * width
    cols = fgate.shape[1]
    k = nz - 1
    vm = pl.BlockSpec(memory_space=VMEM)
    hbm = pl.BlockSpec(memory_space=pl.ANY)
    by_head = (heads, tokens, width)
    saved = [
        ((model, lru), BF16), ((model, lru), BF16), ((lru, model), BF16), ((HALO + tokens, model), BF16),
        ((heads, HALO + tokens, width), F32), (by_head, F32), (by_head, BF16), (by_head, BF16), (by_head, BF16),
        (by_head, F32), ((tokens, lru), BF16), ((3, tokens, model), BF16), ((3, cols, model), BF16),
    ]
    kept = [
        ((1, lru), F32), ((tokens, LANE), F32), ((8, lru), F32), ((tokens, model), F32), ((tokens, model), F32),
        ((1, model), F32),
    ]
    sems = []
    for shape in ((5, k, 2), (3, 2 * k, 8), (2, 2 * k), (4,), (k,), (k,), (1,), (3,), (3,)):
        sems += [DMA(shape)] * 2
    return pl.pallas_call(
        functools.partial(forward_kernel, nz, heads),
        out_shape=tuple(jax.ShapeDtypeStruct(*a) for a in saved + kept),
        in_specs=[vm] * 4 + [hbm] * 7,
        out_specs=[hbm] * len(saved) + [vm] * len(kept),
        scratch_shapes=[
            VMEM((model, lru), BF16), VMEM((model, lru), BF16), VMEM((lru, model), BF16), VMEM((3, cols, model), BF16),
            VMEM((4, tokens, model), BF16), VMEM((2, model, 256), BF16), VMEM((2, 256, model), BF16),
            VMEM((HALO + tokens, model), BF16), VMEM((heads, HALO + tokens, width), F32), VMEM(by_head, F32),
            VMEM(by_head, BF16), VMEM(by_head, BF16), VMEM(by_head, BF16), VMEM(by_head, F32), VMEM((tokens, lru), BF16),
            VMEM(by_head, F32), VMEM((nz, 8, lru), F32), VMEM((8, nz * tokens), F32), VMEM((HALO, model), BF16),
            VMEM((tokens, model), F32), VMEM((4 * tokens, model), BF16), VMEM((4 * tokens, cols), BF16),
            VMEM((4 * tokens, cols), BF16), VMEM((4 * tokens, cols), BF16), VMEM((3, tokens, model), BF16),
            VMEM((3, tokens, model), BF16), VMEM((3, tokens, model), BF16), VMEM((tokens, model), F32),
            DMA((8,)), DMA((len(saved),)),
        ] + sems,
        compiler_params=pltpu.CompilerParams(collective_id=0, has_side_effects=True, vmem_limit_bytes=62 * 2**20),
        name="forward_and_feed",
    )(x, vecs, rg, ig, cot, lw, bw, ow, fgate, fup, fdown)


def backward_kernel(nz, heads, rg, ig, sin, mk, vec, vecs, rgrad, g2g,
                    i_x, i_wl, i_wb, i_wo, i_fb, i_lin, i_br, i_cv, i_rl, i_il, i_st, i_pr, i_base, i_y, i_ffg,
                    wa, fa, ga, bout, igrad, osm, osmz,
                    x, wl, wb, wo, fb, lin, br, cv, rl, il, st, pr, yk, fown,
                    rgb, turned, fl, rlg, ilg, bg, lgr, ends, hal,
                    g, wc, wp, wz, fin, fc, fz, ffin, gt, gc, gp, gz, gfin, sm, smz, yp,
                    lsem, osem, wcs, wcr, wps, wpr, wzs, wzr, was, war, fcs, fcr, fzs, fzr, fas, far,
                    gcs, gcr, gps, gpr, gzs, gzr, gys, gyr, gas, gar, yps, ypr, s1s, s1r, s2s, s2r,
                    es, er, hs, hr):
    me = Place(nz)
    out = Sends()
    core, other, chip, z = me.core, 1 - me.core, me.chip, me.z
    tokens, model = x.shape
    lru = wl.shape[1]
    width = lru // heads
    own = lru // nz
    block = model // 8
    half_rows = block // 2
    part = fc.shape[2]
    k = nz - 1

    loads = dict(
        pr=(i_pr, pr), wo=(i_wo, wo), br=(i_br, br), st=(i_st, st), fown=(i_ffg.at[:, :, core], fown),
        y0=(i_y.at[1, 0:tokens // 2], yk.at[0]), y1=(i_y.at[0, tokens // 2:tokens], yk.at[1]),
        rl=(i_rl, rl), fb=(i_fb, fb), wb=(i_wb, wb), cv=(i_cv, cv), il=(i_il, il), lin=(i_lin, lin), wl=(i_wl, wl),
        x=(i_x, x), base=(i_base, bout),
    )
    loads = {name: pltpu.make_async_copy(a, b, lsem.at[i]) for i, (name, (a, b)) in enumerate(loads.items())}
    for copy in loads.values():
        copy.start()

    def need(*names):
        for name in names:
            loads[name].wait()

    greet([me.along(d) for d in range(1, nz)] + [me.plane(r) for r in (1, 2, 3)] + [me.sibling()])


    def lanes(h):
        return head_lanes(h, width)

    def feed_core():
        return remote(i_ffg.at[:, :, other], fc, fcs.at[0], fcr.at[0], me.sibling())

    def feed_along(d):
        return lambda: remote(fc.at[:, me.along(d)[1]], fz.at[d - 1], fzs.at[d - 1], fzr.at[d - 1], me.along(d))

    def feed_sum():
        out.arrived(feed_core)
        need("fown")

        def add(i, _):
            for m in range(3):
                fc[m, i] = (fc[m, i].astype(F32) + fown[m, i].astype(F32)).astype(BF16)
            return 0

        lax.fori_loop(0, nz, add, 0)
        for d in range(1, nz):
            out.go(feed_along(d))

    def feed_place(c, kk, half):
        at = pl.multiple_of((2 * c + kk) * part, part)
        if half is None:
            return fa.at[:, pl.ds(at, part)]
        return fa.at[:, pl.ds(pl.multiple_of(at + half * (part // 2), part // 2), part // 2)]

    feed_gather = PlaneGather(me, out, feed_place, fas, far, (), None, first=lambda: ffin)
    feed_own = pltpu.make_async_copy(ffin, feed_place(chip, core, None), osem.at[3])

    def feed_total():
        for d in range(1, nz):
            out.arrived(feed_along(d))
        for m in range(3):
            total = fc[m, z].astype(F32)
            for d in range(k):
                total = total + fz[d, m].astype(F32)
            ffin[m] = total.astype(BF16)
        feed_gather.begin()
        feed_own.start()

    def y_half(r, half):
        return i_y.at[r - 1, pl.ds(half * (tokens // 2), tokens // 2)]

    y_sum = PlaneSum(me, out, lambda r, half: yk.at[half], lambda i: yp.at[i], yps, ypr, (), source=y_half)

    slot_of = {2: 0, 1: 1, 0: 0}

    def core_of(m):
        at = pl.ds(pl.multiple_of(other * (model // 2), model // 2), model // 2)
        return lambda: remote(g.at[slot_of[m], at], wc.at[m], wcs.at[m], wcr.at[m], me.sibling())

    core_copies = [core_of(m) for m in range(3)]

    def block_of(m, r, half=None):
        start = me.chip_of(r) * block
        if half is None:
            return wc.at[m, pl.ds(pl.multiple_of(start, block), block)]
        return wc.at[m, pl.ds(pl.multiple_of(start + half * half_rows, half_rows), half_rows)]

    sums = [
        PlaneSum(me, out, lambda r, half, m=m: block_of(m, r, half), lambda i, m=m: wp.at[m, i], wps, wpr, (m,))
        for m in range(3)
    ]

    def core_sum(m):
        out.arrived(core_copies[m])

        def add(c, _):
            at = rows(c, block)
            mine = pl.ds(pl.multiple_of(core * (model // 2) + c * block, block), block)
            wc[m, at, :] = (wc[m, at, :].astype(F32) + g[slot_of[m], mine, :].astype(F32)).astype(BF16)
            return 0

        lax.fori_loop(0, 4, add, 0)
        sums[m].begin()

    def z_copy(m, d):
        return lambda: remote(
            wc.at[m, rows(chip, block), rows(me.along(d)[1], own)], wz.at[m, d - 1], wzs.at[m, d - 1], wzr.at[m, d - 1], me.along(d)
        )

    def plane_total(m):
        for half in range(2):
            at = pl.ds(pl.multiple_of(chip * block + half * half_rows, half_rows), half_rows)
            wc[m, at, :] = (wc[m, at, :].astype(F32) + sums[m].total(half)).astype(BF16)
        for d in range(1, nz):
            out.go(z_copy(m, d))

    def weight_place(m):
        def place(c, kk, half):
            start = (4 * kk + c) * block
            if half is None:
                return wa.at[m, pl.ds(pl.multiple_of(start, block), block)]
            return wa.at[m, pl.ds(pl.multiple_of(start + half * half_rows, half_rows), half_rows)]
        return place

    gathers = [PlaneGather(me, out, weight_place(m), was, war, (m,), None, first=lambda m=m: fin.at[m]) for m in range(3)]
    own_copies = [pltpu.make_async_copy(fin.at[m], weight_place(m)(chip, core, None), osem.at[m]) for m in range(3)]

    def z_total(m):
        for d in range(1, nz):
            out.arrived(z_copy(m, d))
        total = wc[m, rows(chip, block), rows(z, own)].astype(F32)
        for d in range(k):
            total = total + wz[m, d].astype(F32)
        fin[m] = total.astype(BF16)
        gathers[m].begin()
        own_copies[m].start()

    gate_half = gt.shape[0] // 2
    gate_block = gt.shape[0] // 8
    gate_part = gate_block // nz

    def gate_core():
        at = pl.ds(pl.multiple_of(other * gate_half, gate_half), gate_half)
        return remote(gt.at[at], gc, gcs.at[0], gcr.at[0], me.sibling())

    def gate_rows(r, half):
        return gc.at[pl.ds(pl.multiple_of(me.chip_of(r) * gate_block + half * (gate_block // 2), gate_block // 2), gate_block // 2)]

    gate_sum = PlaneSum(me, out, gate_rows, lambda i: gp.at[i], gps, gpr, ())

    def gate_core_sum():
        out.arrived(gate_core)
        mine = pl.ds(pl.multiple_of(core * gate_half, gate_half), gate_half)
        gc[...] = (gc[...].astype(F32) + gt[mine, :].astype(F32)).astype(BF16)
        gate_sum.begin()

    def gate_cut(i):
        return pl.ds(pl.multiple_of(chip * gate_block + i * gate_part, gate_part), gate_part)

    def gate_along(d):
        return lambda: remote(gc.at[gate_cut(me.along(d)[1])], gz.at[d - 1], gzs.at[d - 1], gzr.at[d - 1], me.along(d))

    def gate_back(d, origin):
        return lambda: remote(
            gfin.at[rows(origin(), gate_part)], gfin.at[rows(origin(), gate_part)], gys.at[d - 1], gyr.at[d - 1], me.along(d)
        )

    def gate_total():
        for half in range(2):
            at = pl.ds(pl.multiple_of(chip * gate_block + half * (gate_block // 2), gate_block // 2), gate_block // 2)
            gc[at, :] = (gc[at, :].astype(F32) + gate_sum.total(half)).astype(BF16)
        for d in range(1, nz):
            out.go(gate_along(d))

    def gate_z_total():
        for d in range(1, nz):
            out.arrived(gate_along(d))
        total = gc[gate_cut(z), :].astype(F32)
        for d in range(k):
            total = total + gz[d].astype(F32)
        gfin[rows(z, gate_part), :] = total.astype(BF16)
        for d in range(1, nz):
            out.go(gate_back(d, lambda: z))

    def gate_place(c, kk, half):
        start = (4 * kk + c) * gate_block
        if half is None:
            return ga.at[pl.ds(pl.multiple_of(start, gate_block), gate_block)]
        return ga.at[pl.ds(pl.multiple_of(start + half * (gate_block // 2), gate_block // 2), gate_block // 2)]

    gate_gather = PlaneGather(me, out, gate_place, gas, gar, (), None, first=lambda: gfin)
    gate_own = pltpu.make_async_copy(gfin, gate_place(chip, core, None), osem.at[4])

    def gate_spread():
        for d in range(1, nz):
            out.arrived(gate_back(d, lambda: me.z_from(d)))
        gate_gather.begin()
        gate_own.start()

    def small_copy(i):
        peer = (me.sibling(), me.plane(1), me.plane(2))[i]
        return lambda: remote(sm.at[2 * i], sm.at[2 * i + 1], s1s.at[i], s1r.at[i], peer)

    def small_step(i):
        out.arrived(small_copy(i))
        sm[2 * i + 2] = sm[2 * i] + sm[2 * i + 1]
        if i < 2:
            out.go(small_copy(i + 1))
        else:
            smz[z] = sm[6]
            for d in range(1, nz):
                out.go(small_along(d, lambda: z))

    def small_along(d, origin):
        return lambda: remote(sm.at[6], smz.at[origin()], s2s.at[d - 1], s2r.at[d - 1], me.along(d))


    out.go(feed_core)
    y_sum.begin()
    small = sm.at[0]
    small[...] = jnp.zeros(small.shape, F32)
    small[8:9, 0:model] = g2g[...]
    row = lax.broadcasted_iota(jnp.int32, (8, width), 0)
    rgb[...] = rgrad[...].astype(BF16)
    turned[...] = rgb[...].T
    need("pr")

    def wgrad(slot, right):
        def body(h, _):
            g[slot, :, lanes(h)] = dot(turned[...], right[:, lanes(h)], NN).astype(BF16)
            return 0

        lax.fori_loop(0, heads, body, 0)

    wgrad(0, pr)
    out.go(core_copies[2])
    need("wo", "br", "st")

    def branch_back(h, _):
        pg = dot(rgb[...], wo[lanes(h), :], NT)
        act, slope = gelu_both(br[h])
        bg[:, lanes(h)] = (pg * st[h] * slope).astype(BF16)
        fl[h, 0:tokens] = pg * act
        return 0

    lax.fori_loop(0, heads, branch_back, 0)
    need("fb")
    turned[...] = fb[HALO:, :].T
    wgrad(1, bg)
    out.go(core_copies[1])
    feed_sum()
    core_sum(2)
    need("rl")

    def scan_head(h, _):
        rate = softplus(-vec[4:5, lanes(h)]) * -DECAY_SCALE

        def tile(j, carried):
            later, factor = carried
            i = tokens // 16 - 1 - j
            at = rows(i, 16)
            keep = 1.0 - mk[at, 0:1]
            a = keep * jnp.exp(sigmoid(rl[h, at, :].astype(F32)) * rate)
            sgrad = fl[h, at, :]
            b = a * sgrad
            for t in (1, 0):
                cum, run = tile_scan(a[8 * t:8 * t + 8], b[8 * t:8 * t + 8], row, True)
                run = run + cum * later
                cum = cum * factor
                here = pl.ds(pl.multiple_of(i * 16 + 8 * t, 8), 8)
                last = row == 7
                fl[h, here, :] = sgrad[8 * t:8 * t + 8] + jnp.where(last, later, pltpu.roll(run, 7, 0))
                br[h, here, :] = jnp.where(last, factor, pltpu.roll(cum, 7, 0))
                later, factor = run[0:1], cum[0:1]
            return later, factor

        later, factor = lax.fori_loop(
            0, tokens // 16, tile, (jnp.zeros((1, width), F32), jnp.ones((1, width), F32))
        )
        ends[0, 0:1, lanes(h)] = later
        ends[0, 1:2, lanes(h)] = factor
        return 0

    lax.fori_loop(0, heads, scan_head, 0)

    def end_copy(d):
        return lambda: remote(ends.at[0], ends.at[d], es.at[d - 1], er.at[d - 1], me.along(nz - d))

    for d in range(1, nz):
        out.go(end_copy(d))
    core_sum(1)
    need("wb")
    igrad[...] = jnp.zeros(igrad.shape, F32)

    def first_back(left, right):
        def body(j, _):
            at = rows(j, 256)
            igrad[:, at] += dot(left[...], right[at, :], NT)
            return 0

        lax.fori_loop(0, model // 256, body, 0)

    first_back(bg, wb)
    need("y0", "y1")
    y_sum.relay()
    sums[2].relay()
    for d in range(1, nz):
        out.arrived(end_copy(d))
    incoming = jnp.zeros((1, lru), F32)
    for d in range(nz - 1, 0, -1):
        end = ends[d, 0:1, :] + ends[d, 1:2, :] * incoming
        incoming = jnp.where(d + z < nz, end, incoming)
    sm[1, 0:1, :] = incoming
    need("cv", "il")

    def terms(h, _):
        raw = vec[4:5, lanes(h)]
        soft = softplus(-raw)
        later = sm[1, 0:1, lanes(h)]

        def tile(i, carried):
            before, decays, rates, inputs = carried
            at = rows(i, 16)
            start = mk[at, 0:1]
            keep = 1.0 - start
            flow = fl[h, at, :] + br[h, at, :] * later
            state = st[h, at, :]
            first = lax.broadcasted_iota(jnp.int32, (16, width), 0) == 0
            earlier = jnp.where(first, before, pltpu.roll(state, 1, 0))
            sig = sigmoid(rl[h, at, :].astype(F32))
            gate = sigmoid(il[h, at, :].astype(F32))
            decay = jnp.exp(sig * (soft * -DECAY_SCALE))
            root = jnp.sqrt(1.0 - decay * decay)
            level = start + keep * root
            conv = cv[h, at, :].astype(F32)
            to_scale = flow * conv
            to_decay = keep * (flow * earlier - to_scale * gate * (decay / root))
            to_power = to_decay * decay * sig
            rate_grad = (to_power * (1.0 - sig) * (soft * -DECAY_SCALE)).astype(BF16)
            input_grad = (to_scale * level * gate * (1.0 - gate)).astype(BF16)
            rlg[h, at, :] = rate_grad
            ilg[h, at, :] = input_grad
            fl[h, at, :] = flow * level * gate
            rates = rates + rate_grad.astype(F32)
            inputs = inputs + input_grad.astype(F32)
            return state[15:16], decays + to_power, rates, inputs

        zero = jnp.zeros((16, width), F32)
        _, decays, rates, inputs = lax.fori_loop(0, tokens // 16, tile, (sin[:, lanes(h)], zero, zero, zero))
        small[4:5, lanes(h)] = jnp.sum(decays, axis=0, keepdims=True) * (DECAY_SCALE * sigmoid(-raw))
        small[5:6, lanes(h)] = jnp.sum(rates, axis=0, keepdims=True)
        small[6:7, lanes(h)] = jnp.sum(inputs, axis=0, keepdims=True)
        rate_out, input_out = rlg[h], ilg[h]
        gt[rows(h, width), :] = dot(cv[h], rate_out, TN).astype(BF16)
        gt[rows(heads + h, width), :] = dot(cv[h], input_out, TN).astype(BF16)
        path = (dot(rate_out, rg[h], NT) + dot(input_out, ig[h], NT)).astype(BF16)
        fl[h, 0:tokens] = fl[h, 0:tokens] + path.astype(F32)
        hal[0, h] = fl[h, 0:8]
        return 0

    lax.fori_loop(0, heads, terms, 0)

    def halo():
        return remote(hal.at[0], hal.at[1], hs.at[0], hr.at[0], me.along(nz - 1))

    out.go(halo)
    out.go(gate_core)
    sums[1].relay()
    plane_total(2)
    need("lin")
    out.sent(core_copies[2])
    out.arrived(halo)

    def filter_back(h, _):
        taps = vec[0:4, lanes(h)]
        fl[h, tokens:tokens + 8] = hal[1, h]
        value = taps[0:1] * fl[h, 0:tokens]
        small[0:1, lanes(h)] = jnp.sum(fl[h, 0:tokens] * lin[h, HALO:], axis=0, keepdims=True)
        for t in range(1, 4):
            value = value + taps[t:t + 1] * (fl[h, t:t + tokens] * mk[:, 3 + t:4 + t])
            small[t:t + 1, lanes(h)] = jnp.sum(
                fl[h, 0:tokens] * (lin[h, HALO - t:HALO - t + tokens] * mk[:, t:t + 1]), axis=0, keepdims=True
            )
        lgr[:, lanes(h)] = value.astype(BF16)
        return 0

    lax.fori_loop(0, heads, filter_back, 0)
    wgrad(0, lgr)
    out.go(core_copies[0])
    gate_core_sum()
    need("wl")
    first_back(lgr, wl)
    core_sum(0)
    need("x")
    value = x[...].astype(F32)
    fgrad = igrad[...]
    q = fgrad * vecs[0:1, 0:model]
    inv = lax.rsqrt(jnp.mean(value * value, axis=-1, keepdims=True) + EPS)
    pull = jnp.mean(q * value, axis=-1, keepdims=True)
    small[7:8, 0:model] = jnp.sum(fgrad * value * inv, axis=0, keepdims=True)
    igrad[...] = rgrad[...] + (inv * q - value * (inv * inv * inv * pull))
    out.go(small_copy(0))
    plane_total(1)
    z_total(2)
    feed_total()
    small_step(0)
    gate_sum.relay()
    need("base")
    for half in range(2):
        at = pl.ds(half * (tokens // 2), tokens // 2)
        bout[at, :] = bout[at, :] + y_sum.total(half)
    sums[0].relay()
    small_step(1)
    gathers[2].relay()
    gate_total()
    z_total(1)
    small_step(2)
    plane_total(0)
    gate_z_total()
    feed_gather.relay()
    gathers[2].far()
    gathers[1].relay()
    z_total(0)
    gate_spread()
    gathers[1].far()
    feed_gather.far()
    gathers[0].relay()
    gate_gather.relay()
    for d in range(1, nz):
        out.arrived(small_along(d, lambda: me.z_from(d)))
    total = smz[0]
    for i in range(1, nz):
        total = total + smz[i]
    osm[...] = total
    osmz[...] = osm[:, rows(z, own)]
    gathers[0].far()
    gate_gather.far()
    for gathered in gathers + [feed_gather, gate_gather]:
        gathered.end()
    for copy in own_copies + [feed_own, gate_own]:
        copy.wait()
    out.finish()


def backward(nz, rg, ig, sin, mk, vec, vecs, rgrad, g2g, x, wl, wb, wo, fb, lin, br, cv, rl, il, st, pr, base, y, ffg):
    tokens, model = x.shape
    heads, width = rg.shape[0], rg.shape[1]
    lru = heads * width
    own = lru // nz
    part = ffg.shape[3]
    k = nz - 1
    block = model // 8
    gate_rows = 2 * lru
    gate_block = gate_rows // 8
    vm = pl.BlockSpec(memory_space=VMEM)
    hbm = pl.BlockSpec(memory_space=pl.ANY)
    by_head = (heads, tokens, width)
    half = tokens // 2
    sems = []
    for shape in (
        (3,), (3, 6), (3, k), (3, 8), (1,), (k,), (8,),
        (1,), (6,), (k,), (k,), (8,), (6,), (3,), (k,), (k,), (1,),
    ):
        sems += [DMA(shape)] * 2
    return pl.pallas_call(
        functools.partial(backward_kernel, nz, heads),
        out_shape=(
            jax.ShapeDtypeStruct((3, model, own), BF16),
            jax.ShapeDtypeStruct((3, 8 * part, model), BF16),
            jax.ShapeDtypeStruct((gate_rows, width), BF16),
            jax.ShapeDtypeStruct((tokens, model), F32),
            jax.ShapeDtypeStruct((tokens, model), F32),
            jax.ShapeDtypeStruct((16, lru), F32),
            jax.ShapeDtypeStruct((16, own), F32),
        ),
        in_specs=[vm] * 8 + [hbm] * 15,
        out_specs=[hbm] * 3 + [vm] * 4,
        scratch_shapes=[
            VMEM((tokens, model), BF16), VMEM((model, lru), BF16), VMEM((model, lru), BF16), VMEM((lru, model), BF16),
            VMEM((HALO + tokens, model), BF16), VMEM((heads, HALO + tokens, width), F32), VMEM(by_head, F32),
            VMEM(by_head, BF16), VMEM(by_head, BF16), VMEM(by_head, BF16), VMEM(by_head, F32), VMEM((tokens, lru), BF16),
            VMEM((2, half, model), BF16), VMEM((3, nz, part, model), BF16),
            VMEM((tokens, model), BF16), VMEM((model, tokens), BF16), VMEM((heads, tokens + 8, width), F32),
            VMEM(by_head, BF16), VMEM(by_head, BF16), VMEM((tokens, lru), BF16), VMEM((tokens, lru), BF16),
            VMEM((nz, 8, lru), F32), VMEM((2, heads, 8, width), F32),
            VMEM((2, model, lru), BF16), VMEM((3, model // 2, lru), BF16), VMEM((3, 6, block // 2, lru), BF16),
            VMEM((3, k, block, own), BF16), VMEM((3, block, own), BF16),
            VMEM((3, nz, part, model), BF16), VMEM((k, 3, part, model), BF16), VMEM((3, part, model), BF16),
            VMEM((gate_rows, width), BF16), VMEM((gate_rows // 2, width), BF16), VMEM((6, gate_block // 2, width), BF16),
            VMEM((k, gate_block // nz, width), BF16), VMEM((gate_block, width), BF16),
            VMEM((7, 16, lru), F32), VMEM((nz, 16, lru), F32), VMEM((6, half, model), BF16),
            DMA((16,)), DMA((5,)),
        ] + sems,
        compiler_params=pltpu.CompilerParams(collective_id=1, has_side_effects=True, vmem_limit_bytes=62 * 2**20),
        name="backward_and_sums",
    )(rg, ig, sin, mk, vec, vecs, rgrad, g2g, x, wl, wb, wo, fb, lin, br, cv, rl, il, st, pr, base, y, ffg)


def results_kernel(wa, fa, ga, bout, igrad, osm, osmz,
                   o_out, o_in, o_g1, o_branch, o_lru, o_taps, o_gates, o_rb, o_ib, o_decay, o_ow, o_g2, o_gate, o_up, o_down):
    model = bout.shape[1]

    @pl.when(pl.program_id(0) == 0)
    def _():
        o_out[...] = bout[...]
        o_in[...] = igrad[...]
        o_taps[...] = osmz[0:4, :]
        o_decay[...] = osmz[4:5, :]
        o_rb[...] = osm[5:6, :]
        o_ib[...] = osm[6:7, :]
        o_g1[...] = osm[7:8, 0:model]
        o_g2[...] = osm[8:9, 0:model]

    o_lru[...] = wa[0].astype(F32)
    o_branch[...] = wa[1].astype(F32)
    o_ow[...] = wa[2].T.astype(F32)
    o_gates[...] = ga[...].astype(F32)
    o_gate[...] = fa[0].T.astype(F32)
    o_up[...] = fa[1].T.astype(F32)
    o_down[...] = fa[2].astype(F32)


def results(wa, fa, ga, bout, igrad, osm, osmz):
    steps = 3
    model, own = wa.shape[1:]
    cols = fa.shape[1]
    gate_rows, width = ga.shape
    lru = osm.shape[1]
    tokens = bout.shape[0]

    def whole(shape):
        return pl.BlockSpec(shape, lambda i: (0,) * len(shape))

    across = pl.BlockSpec((model, own // steps), lambda i: (0, i))
    feed_across = pl.BlockSpec((model, cols // steps), lambda i: (0, i))
    outs = [
        ((tokens, model), whole((tokens, model))), ((tokens, model), whole((tokens, model))), ((1, model), whole((1, model))),
        ((model, own), across), ((model, own), across), ((4, own), whole((4, own))),
        ((gate_rows, width), pl.BlockSpec((gate_rows // steps, width), lambda i: (i, 0))),
        ((1, lru), whole((1, lru))), ((1, lru), whole((1, lru))), ((1, own), whole((1, own))),
        ((own, model), pl.BlockSpec((own // steps, model), lambda i: (i, 0))), ((1, model), whole((1, model))),
        ((model, cols), feed_across), ((model, cols), feed_across),
        ((cols, model), pl.BlockSpec((cols // steps, model), lambda i: (i, 0))),
    ]
    return pl.pallas_call(
        results_kernel,
        grid=(steps,),
        out_shape=tuple(jax.ShapeDtypeStruct(shape, F32) for shape, _ in outs),
        in_specs=[
            pl.BlockSpec((3, model, own // steps), lambda i: (0, 0, i)),
            pl.BlockSpec((3, cols // steps, model), lambda i: (0, i, 0)),
            pl.BlockSpec((gate_rows // steps, width), lambda i: (i, 0)),
            whole((tokens, model)), whole((tokens, model)), whole((16, lru)), whole((16, own)),
        ],
        out_specs=tuple(spec for _, spec in outs),
        compiler_params=pltpu.CompilerParams(vmem_limit_bytes=48 * 2**20),
        name="results",
    )(wa, fa, ga, bout, igrad, osm, osmz)


def local(
    nz,
    groups,
    block_input,
    doc_starts,
    first_gain,
    branch_weight,
    lru_weight,
    filter_taps,
    rate_gate,
    input_gate,
    rate_bias,
    input_bias,
    decay_logit,
    out_weight,
    second_gain,
    feed_gate,
    feed_up,
    feed_down,
    cotangent,
):
    model = block_input.shape[1]
    heads, width = rate_gate.shape[:2]
    lru = heads * width

    def line(v):
        v = v.astype(F32)
        v = v[None] if v.ndim == 1 else v
        return jnp.pad(v, ((0, 0), (0, lru - v.shape[1])))

    blank = jnp.zeros((3, lru), F32)
    vecs = jnp.concatenate([
        line(first_gain), line(second_gain), line(rate_bias), line(input_bias), line(doc_starts), blank,
        line(filter_taps), line(decay_logit), blank,
    ])
    (wl, wb, wo, fb, lin, br, cv, rl, il, st, pr, y, ffg, sin, mk, vec, base, rgrad, g2g) = forward(
        nz, block_input, vecs, rate_gate, input_gate, cotangent, lru_weight, branch_weight, out_weight,
        feed_gate, feed_up, feed_down,
    )
    ffg = ffg.reshape(3, nz, 2, ffg.shape[1] // (2 * nz), model)
    sums = backward(
        nz, rate_gate, input_gate, sin, mk, vec, vecs, rgrad, g2g, block_input, wl, wb, wo, fb, lin, br, cv, rl, il, st, pr,
        base, y, ffg,
    )
    made = results(*sums)
    block_output, input_grad, *summed = made
    if groups > 1:
        same = [[8 * g + b for g in range(groups)] for b in range(8)]
        summed = lax.psum(tuple(summed), "tp", axis_index_groups=same)
    g1, branch, lru_grad, taps, gates, rb, ib, decay, ow, g2, gate, up, down = summed
    gates = gates.reshape(2, heads, width, width)
    return (
        block_output, input_grad, g1[0], branch, lru_grad, taps, gates[0], gates[1], rb[0], ib[0], decay[0], ow, g2[0],
        gate, up, down,
    )


def solution(mesh):
    by_rows = P(("tp", "dp"), None)
    by_cols = P(None, "dp")
    split = P("dp", None)
    return jax.shard_map(
        functools.partial(local, mesh.shape["dp"], mesh.shape["tp"] // 8),
        mesh=mesh,
        in_specs=(
            by_rows, P("tp"), P(), by_cols, by_cols, by_cols, P(), P(), P(), P(), P("dp"), split, P(), by_cols, by_cols,
            split, by_rows,
        ),
        out_specs=(
            by_rows, by_rows, P(), by_cols, by_cols, by_cols, P(), P(), P(), P(), P("dp"), split, P(), by_cols, by_cols,
            split,
        ),
        check_vma=False,
    )
```

time: 1450 us -> 320 us (0.22); the launches traced: 1430 us -> 318 us
  waiting for transfers between devices: 780 us -> 0 us
  Pallas kernels: 0 us -> 299 us
  local copies, waits for them, and re-layouts: 302 us -> 15.7 us
  other arithmetic: 143 us -> 3.23 us
  blocking collectives: 98.5 us -> 0 us
  matrix products: 64.5 us -> 0 us
  starting transfers between devices: 25.6 us -> 0 us
  between operations: 16.3 us -> 0.69 us
    pallas_call x0 -> x3, Pallas kernels: none -> 299 us  [the longest x1 158 us: backward(): pl.pallas_call(functools.partial(backward_kernel, nz, heads), out_shape=(...]
    reduce_scatter x4 -> x0, waiting for transfers between devices: 257 us -> none  [tokens_out(): lax.psum_scatter(jnp.einsum(form, left, right, preferred_element_type=jnp...]
    psum x2 -> x0, waiting for transfers between devices: 255 us -> none  [the longest x1 194 us: local(): lax.psum((both_proj_wgrad[:, :channels], both_proj_wgrad[:, channels:], t...]
    all_gather x4 -> x0, waiting for transfers between devices: 198 us -> none  [tokens_in(): return lax.all_gather(stacked, 'dp', axis=1, tiled=True)]
    slice x78 -> x1, local copies, waits for them, and re-layouts: 108 us -> 3.74 us  [local(): gates[1]]
    all_to_all x3 -> x0, waiting for transfers between devices: 68.7 us -> none  [the longest x2 53.7 us: to_channels(): lax.all_to_all(stacked, 'dp', split_axis=2, concat_axis=1, tiled=True)]
    dot_general x15 -> x0, matrix products: 64.5 us -> none  [the longest x4 17.6 us: tokens_out(): jnp.einsum(form, left, right, preferred_element_type=jnp.float32)]
    psum x2 -> x0, blocking collectives: 59.6 us -> none  [the longest x1 44.1 us: local(): lax.psum((gate_wgrads[0], gate_wgrads[1], bias_grads[0], bias_grads[1], f...]
  transfers between devices with their start and end apart: 13 -> 0, of which waited for: 13 -> 0; matrix products, arithmetic and copies ran while one was open for 8% -> 0% of each run, Pallas kernels for 0% -> 0%
where the time goes in v1:
time: 320 us; the launch traced here: 318 us
  Pallas kernels  299 us (93%)
  local copies, waits for them, and re-layouts  15.7 us (5%)
  other arithmetic  3.23 us (1%)
    pallas_call x1, Pallas kernels, backward(): pl.pallas_call(functools.partial(backward_kernel, nz, heads), out_shape=(...  158 us
    pallas_call x1, Pallas kernels, forward(): pl.pallas_call(functools.partial(forward_kernel, nz, heads), out_shape=tu...  132 us
    pallas_call x1, Pallas kernels, results(): pl.pallas_call(results_kernel, grid=(steps,), out_shape=tuple((jax.ShapeD...  8.52 us
    unnamed x12, local copies, waits for them, and re-layouts  7.14 us

profile of v1, /device:TPU:1, one launch (start us, length us, event | category | flops | bytes accessed | tf_op | source)
XLA Modules:
  0.0 318.1 jit_solution(10644041700095812645)
XLA Ops:
  0.6 0.7 broadcast_in_dim.38
  1.3 0.7 convert_element_type.8
  2.0 0.7 broadcast_in_dim.30
  2.7 0.7 broadcast_in_dim.31
  3.4 0.7 reshape.41
  4.1 0.7 reshape.42
  4.8 0.7 pad_convert_fusion
  5.5 1.3 concatenate.3.vecs
  6.8 131.6 %forward_and_feed.1 = (bf16[1024,1536]{1,0:T(8,128)(2,1)}, bf16[1024,1536]{1,0:T(8,128)(2,1)}, bf16[1536,1024]{1,0:T(8,128)(2,1)}, bf16[272,1024]{1,0:T(8,128)(2...) custom-call(bf16[256,1024]{1,0:T(8,128)(2,1)} %i_x.1, ...), custom_call_target="tpu_custom_call" | custom-call | tf_op jit(solution)/shard_map/forward_and_feed/pallas_call | solution.py:670
  138.5 158.3 %backward_and_sums.1 = (bf16[3,1024,384]{2,1,0:T(8,128)(2,1)}, bf16[3,768,1024]{2,1,0:T(8,128)(2,1)}, bf16[3072,256]{1,0:T(8,128)(2,1)}, f32[256,1024]{1,0:T(8,1...) custom-call(bf16[6,256,256]{2,1,0:T(8,128)(2,1)} %rg.3, bf16[6,256,256]{2,1,0:T(8,128)(2,1)} %ig.3, ...), custom_call_target="tpu_custom_call" | custom-call | tf_op jit(solution)/shard_map/backward_and_sums/pallas_call | solution.py:1167
  296.8 0.0 copy-start
  296.8 1.7 copy-done
  298.5 0.0 copy-start.1
  298.5 1.4 copy-done.1
  299.9 0.0 copy-start.2
  299.9 1.2 copy-done.2
  301.1 0.0 copy-start.3
  301.1 1.2 copy-done.3
  302.4 0.0 copy-start.4
  302.4 0.9 copy-done.4
  303.3 0.0 copy-start.5
  303.3 0.7 copy-done.5
  304.0 8.5 %results.1 = (f32[256,1024]{1,0:T(8,128)}, f32[256,1024]{1,0:T(8,128)}, f32[1,1024]{1,0:T(1,128)}, f32[1024,384]{1,0:T(8,128)}, f32[1024,384]{1,0:T(8,128)}, /*i...) custom-call(bf16[3,1024,384]{2,1,0:T(8,128)(2,1)S(1)} %copy-done, ...), custom_call_target="tpu_custom_call" | custom-call | tf_op jit(solution)/shard_map/results/pallas_call | solution.py:1247
  312.5 0.6 reduce.2
  313.1 0.6 reduce
  313.7 0.6 reduce.1
  314.3 3.7 %fusion = (f32[1536,256]{1,0:T(8,128)}, f32[1536,256]{1,0:T(8,128)}) fusion(f32[3072,256]{1,0:T(8,128)} %get-tuple-element.89), kind=kLoop, calls=%fused_computation.4 | loop fusion | bytes 6291456 | tf_op jit(solution)/shard_map/slice | solution.py:1315
  (4 shorter events, 0.0 us)
Async XLA Ops:
  296.8 1.7 copy-start
  298.5 1.4 copy-start.1
  299.9 1.2 copy-start.2
  301.1 1.2 copy-start.3
  302.4 0.9 copy-start.4
  303.3 0.7 copy-start.5
